TPU v7x, 128 devices: a whole 4x4x4 slice. The times are simulated.
128 devices in a mesh: batch: 2 (over core), member: 16 (over y, x), tensor: 4 (over z).
Axes of the slice: x: 4, y: 4, z: 4, core: 2. Of those that a mesh axis runs over, the one named last changes fastest.
Arguments:
- rows_in: bfloat16 [2048, 1536], P(('batch', 'member', 'tensor')), may hold values from -6 to 6
- target: bfloat16 [2048, 1536], P(('batch', 'member'), 'tensor'), may hold values from -6 to 6
- w_in: bfloat16 [16, 1536, 4096], P('member', None, 'tensor'), may hold values from -0.15309311 to 0.15309311, as said below
- w_out: bfloat16 [16, 4096, 1536], P('member', 'tensor'), may hold values from -0.09375 to 0.09375, as said below
Outputs:
- reward: float32 [2048], P(('batch', 'member', 'tensor'))
- grad_in: float32 [16, 1536, 4096], P('member', 'batch', 'tensor')
- grad_out: float32 [16, 4096, 1536], P('member', 'tensor', 'batch')
Inputs may be any that keep to these rules, and one draw needn't show every extreme that they name: `w_in`: each entry lies within the stated bounds. `w_out`: each entry lies within the stated bounds.
All inputs are finite; a program needn't handle non-finite values.
Results may differ from a plain program's by a relative error of at most 0.0035.
The roundings to bfloat16 on the way count: a program that leaves them out, or rounds other values in their place, can miss the bound.
Values may be sent and summed in bfloat16 or wider, within the bound.
A program may use at most 128 MiB of HBM per device.

v0:
```python
import jax
import jax.numpy as jnp
from jax import lax
from jax.sharding import PartitionSpec as P


def silu_slope(pre_act):
    sigmoid = jax.nn.sigmoid(pre_act)
    return sigmoid * (1.0 + pre_act * (1.0 - sigmoid))


def per_device(rows_in, target, w_in, w_out):
    own_rows = rows_in.shape[0]
    gathered = lax.all_gather(rows_in, ("member", "tensor"), axis=0, tiled=True)
    targets_here = lax.all_gather(target, "member", axis=0, tiled=True)
    group_rows = gathered.shape[0]
    local_count = w_in.shape[0]
    members_all = local_count * lax.axis_size("member")
    width_all = w_out.shape[2]
    loss_scale = float(group_rows * lax.axis_size("batch")) ** (-0.5)
    pre_act = jnp.einsum("gf,mfh->mgh", gathered, w_in, preferred_element_type=jnp.float32)
    hidden = jax.nn.silu(pre_act).astype(jnp.bfloat16)
    partial_out = jnp.einsum("mgh,mhf->mgf", hidden, w_out, preferred_element_type=jnp.float32)
    predicted = lax.psum_scatter(partial_out, "tensor", scatter_dimension=2, tiled=True)
    errors = ((predicted - targets_here.astype(jnp.float32)[None]) * loss_scale).astype(
        jnp.bfloat16
    )
    errors_full = lax.all_gather(errors, "tensor", axis=2, tiled=True)
    own_block = lax.axis_index("member") * lax.axis_size("tensor") + lax.axis_index("tensor")
    summed = lax.psum(jnp.sum(predicted, 0).astype(jnp.bfloat16), "member").astype(jnp.float32)
    member_mean = summed / members_all
    spread = jnp.sum((predicted - member_mean[None]) ** 2, axis=(0, 2))
    spread = lax.psum(spread, ("member", "tensor"))
    reward_rows = spread / (members_all * width_all)
    reward = lax.dynamic_slice_in_dim(reward_rows, own_block * own_rows, own_rows, 0)
    grad_out_part = jnp.einsum(
        "mgh,mgf->mhf", hidden, errors_full, preferred_element_type=jnp.float32
    )
    back_grad = jnp.einsum("mgf,mhf->mgh", errors_full, w_out, preferred_element_type=jnp.float32)
    pre_grad = (back_grad * silu_slope(pre_act)).astype(jnp.bfloat16)
    grad_in_part = jnp.einsum("gf,mgh->mfh", gathered, pre_grad, preferred_element_type=jnp.float32)
    grad_in, grad_out = (
        lax.psum_scatter(grad_in_part, "batch", scatter_dimension=1, tiled=True),
        lax.psum_scatter(grad_out_part, "batch", scatter_dimension=2, tiled=True),
    )
    return (reward, grad_in, grad_out)


def solution(mesh):
    return jax.shard_map(
        per_device,
        mesh=mesh,
        in_specs=(
            P(("batch", "member", "tensor"), None),
            P(("batch", "member"), "tensor"),
            P("member", None, "tensor"),
            P("member", "tensor", None),
        ),
        out_specs=(
            P(("batch", "member", "tensor")),
            P("member", "batch", "tensor"),
            P("member", "tensor", "batch"),
        ),
        check_vma=False,
    )
```

profile of v0, /device:TPU:0, one launch (start us, length us, event | category | flops | bytes accessed | tf_op | source)
XLA Modules:
  0.0 499.6 jit_solution(12518371583038524889)
XLA Ops:
  7.2 0.0 copy-start
  7.2 0.0 all-gather.3.cloned.1.call-start
  7.2 0.7 all-gather.3.cloned.1.call-update
  7.9 0.0 reduce-scatter.4.cloned.1.call-start
  8.0 72.5 %all-gather.3.cloned.1.call-done = bf16[1024,1536]{1,0:T(8,128)(2,1)} async-done(((bf16[16,1536]{1,0:T(8,128)(2,1)}), bf16[1024,1536]{1,0:T(8,128)(2,1)}) %all-gather.3.cloned.1.call-update) | async-done | bytes 3145744 | tf_op jit(solution)/shard_map/all_gather | solution.py:14
  80.4 6.3 %fusion.12 = f32[1024,1024]{1,0:T(8,128)S(1)} fusion(bf16[1024,1536]{1,0:T(8,128)(2,1)} %all-gather.3.cloned.1.call-done, bf16[1,1536,1024]{2,1,0:T(8,128)(2,1)} %param.6), kind=kOutput, calls=%fused_computation.19 | convolution fusion | flops 3221225472 | bytes 10485760 | tf_op jit(solution)/shard_map/gf,mfh->mgh/dot_general | solution.py:21
  86.7 0.0 copy-start.2
  86.8 1.9 copy-done.2
  88.7 0.0 copy-done
  88.7 5.4 %convolution_bitcast_fusion.2 = f32[1,1024,1536]{2,1,0:T(8,128)} fusion(bf16[1,1024,1536]{2,1,0:T(8,128)(2,1)S(1)} %copy-done, f32[1024,1024]{1,0:T(8,128)S(1)} %fusion.12), kind=kOutput, calls=%fused_computation.2 | convolution fusion | flops 3226468352 | bytes 13631488 | tf_op jit(solution)/shard_map/mgh,mhf->mgf/dot_general | solution.py:23
  94.1 0.0 reduce-scatter.4.cloned.1.call-update
  94.1 0.0 copy-start.1
  94.1 0.0 all-reduce.2.cloned.1.call-start
  94.2 61.8 %reduce-scatter.4.cloned.1.call-done = f32[1,1024,384]{2,1,0:T(8,128)} async-done(((f32[1,1024,1536]{2,1,0:T(8,128)}), f32[1,1024,384]{2,1,0:T(8,128)}) %reduce-scatter.4.cloned.1.call-update) | async-done | bytes 1572880 | tf_op jit(solution)/shard_map/reduce_scatter | solution.py:24
  156.0 2.4 convert_bitcast_fusion
  158.4 0.0 all-reduce.2.cloned.1.call-update
  158.4 0.0 all-gather.5.cloned.1.call-start
  158.5 0.0 copy-done.1
  158.5 27.0 %all_gather.10 = bf16[1024,384]{1,0:T(8,128)(2,1)} all-gather(bf16[64,384]{1,0:T(8,128)(2,1)S(1)} %copy-done.1), channel_id=1, replica_groups=mesh['batch'=2,'member'=16,'tensor'=4] {'member'}, dimensions={0}, use_global_device_ids=true | all-gather | bytes 835584 | tf_op jit(solution)/shard_map/all_gather | solution.py:15
  185.4 60.7 %all-reduce.2.cloned.1.call-done = bf16[1024,384]{1,0:T(8,128)(2,1)} async-done(((bf16[1024,384]{1,0:T(8,128)(2,1)}), bf16[1024,384]{1,0:T(8,128)(2,1)}) %all-reduce.2.cloned.1.call-update) | async-done | bytes 786448 | tf_op jit(solution)/shard_map/psum | solution.py:30
  246.2 3.2 fusion.19
  249.3 0.0 all-gather.5.cloned.1.call-update
  249.4 0.0 reduce-scatter.6.cloned.1.call-start
  249.4 39.1 %all-gather.5.cloned.1.call-done = bf16[1,1024,1536]{2,1,0:T(8,128)(2,1)} async-done(((bf16[1,1024,384]{2,1,0:T(8,128)(2,1)}), bf16[1,1024,1536]{2,1,0:T(8,128)(2,1)}) %all-gather.5.cloned.1.call-update) | async-done | bytes 3145744 | tf_op jit(solution)/shard_map/all_gather | solution.py:28
  288.6 13.7 %convolution_bitcast_fusion.1 = f32[1,1536,1024]{1,2,0:T(8,128)} fusion(bf16[1024,1536]{1,0:T(8,128)(2,1)} %all-gather.3.cloned.1.call-done, f32[1024,1024]{1,0:T(8,128)} %copy-done.2, bf16[1,1024,1536]{2,1,0:T(8,128)(2,1)} %all-gather.5.cloned.1.call-done, bf16[1,1024,1536]{2,1,0:T(8,128)(2,1)S(1)} %copy-done), kind=kOutput, calls=%fused_computation.1 | convolution fusion | flops 6451888128 | bytes 19922944 | tf_op jit(solution)/shard_map/gf,mgh->mfh/dot_general | solution.py:41
  302.2 0.0 reduce-scatter.6.cloned.1.call-update
  302.3 0.2 reduce-scatter.8.cloned.1.call-start
  302.5 9.7 %convolution_bitcast_fusion = f32[1,1024,1536]{2,1,0:T(8,128)} fusion(bf16[1,1024,1536]{2,1,0:T(8,128)(2,1)} %all-gather.5.cloned.1.call-done, f32[1024,1024]{1,0:T(8,128)} %copy-done.2), kind=kOutput, calls=%fused_computation | convolution fusion | flops 3226468352 | bytes 13631488 | tf_op jit(solution)/shard_map/mgh,mgf->mhf/dot_general | solution.py:36
  312.2 0.0 reduce-scatter.8.cloned.1.call-update
  312.2 176.4 %psum.15 = f32[1024]{0:T(1024)S(1)} all-reduce(f32[1024]{0:T(1024)S(1)} %get-tuple-element.7), channel_id=1, replica_groups=mesh['batch'=2,'member'=16,'tensor'=4] {'member','tensor'}, use_global_device_ids=true, to_apply=%region_3.4 | all-reduce | flops 1024 | bytes 8192 | tf_op jit(solution)/shard_map/psum | solution.py:33
  488.6 0.6 dynamic_slice.3
  489.2 0.0 reduce-scatter.6.cloned.1.call-done
  489.2 3.5 copy.8
  492.7 0.0 reduce-scatter.8.cloned.1.call-done
  (1 shorter events, 0.0 us)
Async XLA Ops:
  7.2 81.5 %copy-start = (bf16[1,1024,1536]{2,1,0:T(8,128)(2,1)S(1)}, bf16[1,1024,1536]{2,1,0:T(8,128)(2,1)}, u32[]{:S(2)}) copy-start(bf16[1,1024,1536]{2,1,0:T(8,128)(2,1)} %param.7) | copy-start | bytes 9437188
  7.2 73.3 %all-gather.3.cloned.1.call-start = ((), (), s32[]{:S(2)}) async-start(), calls=%async_computation.3 | async-start | bytes 3194880 | tf_op jit(solution)/shard_map/all_gather | solution.py:14
  7.9 148.1 %reduce-scatter.4.cloned.1.call-start = ((), (), s32[]{:S(2)}) async-start(), calls=%async_computation.4 | async-start | bytes 7864320 | tf_op jit(solution)/shard_map/reduce_scatter | solution.py:24
  86.7 1.9 copy-start.2
  94.1 64.4 %copy-start.1 = (bf16[64,384]{1,0:T(8,128)(2,1)S(1)}, bf16[64,384]{1,0:T(8,128)(2,1)}, u32[]{:S(2)}) copy-start(bf16[64,384]{1,0:T(8,128)(2,1)} %param.5) | copy-start | bytes 147460
  94.1 152.0 %all-reduce.2.cloned.1.call-start = ((), (), s32[]{:S(2)}) async-start(), calls=%async_computation.5 | async-start | bytes 1572864 | tf_op jit(solution)/shard_map/psum | solution.py:30
  158.4 130.1 %all-gather.5.cloned.1.call-start = ((), (), s32[]{:S(2)}) async-start(), calls=%async_computation.6 | async-start | bytes 3932160 | tf_op jit(solution)/shard_map/all_gather | solution.py:28
  249.4 239.8 %reduce-scatter.6.cloned.1.call-start = ((), (), s32[]{:S(2)}) async-start(), calls=%async_computation.7 | async-start | bytes 9437184 | tf_op jit(solution)/shard_map/reduce_scatter | solution.py:43
  302.3 190.5 %reduce-scatter.8.cloned.1.call-start = ((), (), s32[]{:S(2)}) async-start(), calls=%async_computation.8 | async-start | bytes 9437184 | tf_op jit(solution)/shard_map/reduce_scatter | solution.py:44
Sparse Core Ops, SparseCore 0:
  10.9 69.5 all-gather.2
  94.3 61.7 reduce-scatter.3
  159.9 86.2 all-reduce.1
  249.5 39.0 all-gather.4
  302.4 17.1 reduce-scatter.5
  322.4 18.5 reduce-scatter.7
where the time goes:
time: 500 us
  waiting for transfers between devices  235 us (47%)
  blocking collectives  203 us (41%)
  matrix products  35.1 us (7%)
  between operations  14.2 us (3%)
  local copies, waits for them, and re-layouts  6.07 us (1%)
  other arithmetic  5.53 us (1%)
    psum x1, blocking collectives, per_device(): spread = lax.psum(spread, ('member', 'tensor'))  176 us
    all_gather x1, waiting for transfers between devices, per_device(): gathered = lax.all_gather(rows_in, ('member', 'tensor'), axis=0, tiled=True)  72.5 us
    reduce_scatter x1, waiting for transfers between devices, per_device(): lax.psum_scatter(partial_out, 'tensor', scatter_dimension=2, tiled=True)  61.8 us
    psum x1, waiting for transfers between devices, per_device(): lax.psum(jnp.sum(predicted, 0).astype(jnp.bfloat16), 'member')  60.7 us
    all_gather x1, waiting for transfers between devices, per_device(): errors_full = lax.all_gather(errors, 'tensor', axis=2, tiled=True)  39.1 us
    all_gather x1, blocking collectives, per_device(): targets_here = lax.all_gather(target, 'member', axis=0, tiled=True)  27 us
    dot_general x1, matrix products, per_device(): jnp.einsum('gf,mgh->mfh', gathered, pre_grad, preferred_element_type=jnp....  13.7 us
  transfers between devices with their start and end apart: 6, of which 4 were waited for; matrix products, arithmetic and copies ran while one was open for 3% of the time, Pallas kernels for 0%

commit v1 on v0

--- a/solution.py
+++ b/solution.py
@@ -30,7 +30,7 @@
     summed = lax.psum(jnp.sum(predicted, 0).astype(jnp.bfloat16), "member").astype(jnp.float32)
     member_mean = summed / members_all
     spread = jnp.sum((predicted - member_mean[None]) ** 2, axis=(0, 2))
-    spread = lax.psum(spread, ("member", "tensor"))
+    spread = lax.psum(lax.psum(spread, "member"), "tensor")
     reward_rows = spread / (members_all * width_all)
     reward = lax.dynamic_slice_in_dim(reward_rows, own_block * own_rows, own_rows, 0)
     grad_out_part = jnp.einsum(

time: 500 us -> 372 us (0.74)
  blocking collectives: 203 us -> 75.3 us
    psum x1 -> x2, blocking collectives: 176 us -> 48.4 us  [per_device(): spread = lax.psum(lax.psum(spread, 'member'), 'tensor')]
  transfers between devices with their start and end apart: 6 -> 6, of which waited for: 4 -> 4; matrix products, arithmetic and copies ran while one was open for 3% -> 4% of each run, Pallas kernels for 0% -> 0%
where the time goes in v1:
time: 372 us
  waiting for transfers between devices  235 us (63%)
  blocking collectives  75.3 us (20%)
  matrix products  35.1 us (9%)
  between operations  14.2 us (4%)
  local copies, waits for them, and re-layouts  6.08 us (2%)
  other arithmetic  5.53 us (1%)
    all_gather x1, waiting for transfers between devices, per_device(): gathered = lax.all_gather(rows_in, ('member', 'tensor'), axis=0, tiled=True)  72.5 us
    reduce_scatter x1, waiting for transfers between devices, per_device(): lax.psum_scatter(partial_out, 'tensor', scatter_dimension=2, tiled=True)  61.8 us
    psum x1, waiting for transfers between devices, per_device(): lax.psum(jnp.sum(predicted, 0).astype(jnp.bfloat16), 'member')  60.8 us
    psum x2, blocking collectives, per_device(): spread = lax.psum(lax.psum(spread, 'member'), 'tensor')  48.4 us
    all_gather x1, waiting for transfers between devices, per_device(): errors_full = lax.all_gather(errors, 'tensor', axis=2, tiled=True)  39.1 us
    all_gather x1, blocking collectives, per_device(): targets_here = lax.all_gather(target, 'member', axis=0, tiled=True)  26.9 us
    dot_general x1, matrix products, per_device(): jnp.einsum('gf,mgh->mfh', gathered, pre_grad, preferred_element_type=jnp....  13.7 us
    dot_general x1, matrix products, per_device(): jnp.einsum('mgh,mgf->mhf', hidden, errors_full, preferred_element_type=jn...  9.72 us
  transfers between devices with their start and end apart: 6, of which 4 were waited for; matrix products, arithmetic and copies ran while one was open for 4% of the time, Pallas kernels for 0%

profile of v1, /device:TPU:0, one launch (start us, length us, event | category | flops | bytes accessed | tf_op | source)
XLA Modules:
  0.0 371.6 jit_solution(1223727932911129981)
XLA Ops:
  7.2 0.0 copy-start
  7.2 0.0 all-gather.3.cloned.1.call-start
  7.2 0.7 all-gather.3.cloned.1.call-update
  7.9 0.0 reduce-scatter.4.cloned.1.call-start
  8.0 72.5 %all-gather.3.cloned.1.call-done = bf16[1024,1536]{1,0:T(8,128)(2,1)} async-done(((bf16[16,1536]{1,0:T(8,128)(2,1)}), bf16[1024,1536]{1,0:T(8,128)(2,1)}) %all-gather.3.cloned.1.call-update) | async-done | bytes 3145744 | tf_op jit(solution)/shard_map/all_gather | solution.py:14
  80.4 6.3 %fusion.12 = f32[1024,1024]{1,0:T(8,128)S(1)} fusion(bf16[1024,1536]{1,0:T(8,128)(2,1)} %all-gather.3.cloned.1.call-done, bf16[1,1536,1024]{2,1,0:T(8,128)(2,1)} %param.6), kind=kOutput, calls=%fused_computation.19 | convolution fusion | flops 3221225472 | bytes 10485760 | tf_op jit(solution)/shard_map/gf,mfh->mgh/dot_general | solution.py:21
  86.7 0.0 copy-start.2
  86.8 1.9 copy-done.2
  88.7 0.0 copy-done
  88.7 5.4 %convolution_bitcast_fusion.2 = f32[1,1024,1536]{2,1,0:T(8,128)} fusion(bf16[1,1024,1536]{2,1,0:T(8,128)(2,1)S(1)} %copy-done, f32[1024,1024]{1,0:T(8,128)S(1)} %fusion.12), kind=kOutput, calls=%fused_computation.2 | convolution fusion | flops 3226468352 | bytes 13631488 | tf_op jit(solution)/shard_map/mgh,mhf->mgf/dot_general | solution.py:23
  94.1 0.0 reduce-scatter.4.cloned.1.call-update
  94.2 0.0 copy-start.1
  94.2 0.0 all-reduce.2.cloned.1.call-start
  94.2 61.8 %reduce-scatter.4.cloned.1.call-done = f32[1,1024,384]{2,1,0:T(8,128)} async-done(((f32[1,1024,1536]{2,1,0:T(8,128)}), f32[1,1024,384]{2,1,0:T(8,128)}) %reduce-scatter.4.cloned.1.call-update) | async-done | bytes 1572880 | tf_op jit(solution)/shard_map/reduce_scatter | solution.py:24
  156.1 2.4 convert_bitcast_fusion
  158.4 0.0 all-reduce.2.cloned.1.call-update
  158.5 0.0 all-gather.5.cloned.1.call-start
  158.5 0.0 copy-done.1
  158.5 26.9 %all_gather.10 = bf16[1024,384]{1,0:T(8,128)(2,1)} all-gather(bf16[64,384]{1,0:T(8,128)(2,1)S(1)} %copy-done.1), channel_id=1, replica_groups=mesh['batch'=2,'member'=16,'tensor'=4] {'member'}, dimensions={0}, use_global_device_ids=true | all-gather | bytes 835584 | tf_op jit(solution)/shard_map/all_gather | solution.py:15
  185.5 60.8 %all-reduce.2.cloned.1.call-done = bf16[1024,384]{1,0:T(8,128)(2,1)} async-done(((bf16[1024,384]{1,0:T(8,128)(2,1)}), bf16[1024,384]{1,0:T(8,128)(2,1)}) %all-reduce.2.cloned.1.call-update) | async-done | bytes 786448 | tf_op jit(solution)/shard_map/psum | solution.py:30
  246.2 3.2 fusion.19
  249.4 0.0 all-gather.5.cloned.1.call-update
  249.4 0.0 reduce-scatter.6.cloned.1.call-start
  249.5 39.1 %all-gather.5.cloned.1.call-done = bf16[1,1024,1536]{2,1,0:T(8,128)(2,1)} async-done(((bf16[1,1024,384]{2,1,0:T(8,128)(2,1)}), bf16[1,1024,1536]{2,1,0:T(8,128)(2,1)}) %all-gather.5.cloned.1.call-update) | async-done | bytes 3145744 | tf_op jit(solution)/shard_map/all_gather | solution.py:28
  288.6 13.7 %convolution_bitcast_fusion.1 = f32[1,1536,1024]{1,2,0:T(8,128)} fusion(bf16[1024,1536]{1,0:T(8,128)(2,1)} %all-gather.3.cloned.1.call-done, f32[1024,1024]{1,0:T(8,128)} %copy-done.2, bf16[1,1024,1536]{2,1,0:T(8,128)(2,1)} %all-gather.5.cloned.1.call-done, bf16[1,1024,1536]{2,1,0:T(8,128)(2,1)S(1)} %copy-done), kind=kOutput, calls=%fused_computation.1 | convolution fusion | flops 6451888128 | bytes 19922944 | tf_op jit(solution)/shard_map/gf,mgh->mfh/dot_general | solution.py:41
  302.3 0.0 reduce-scatter.6.cloned.1.call-update
  302.3 0.2 reduce-scatter.8.cloned.1.call-start
  302.5 9.7 %convolution_bitcast_fusion = f32[1,1024,1536]{2,1,0:T(8,128)} fusion(bf16[1,1024,1536]{2,1,0:T(8,128)(2,1)} %all-gather.5.cloned.1.call-done, f32[1024,1024]{1,0:T(8,128)} %copy-done.2), kind=kOutput, calls=%fused_computation | convolution fusion | flops 3226468352 | bytes 13631488 | tf_op jit(solution)/shard_map/mgh,mgf->mhf/dot_general | solution.py:36
  312.3 0.0 reduce-scatter.8.cloned.1.call-update
  312.3 40.2 %psum.22 = f32[1024]{0:T(1024)S(1)} all-reduce(f32[1024]{0:T(1024)S(1)} %get-tuple-element.7), channel_id=1, replica_groups=mesh['batch'=2,'member'=16,'tensor'=4] {'member'}, use_global_device_ids=true, to_apply=%region_3.4 | all-reduce | flops 1024 | bytes 8192 | tf_op jit(solution)/shard_map/psum | solution.py:33
  352.5 8.1 %psum.23 = f32[1024]{0:T(1024)S(1)} all-reduce(f32[1024]{0:T(1024)S(1)} %psum.22), channel_id=1, replica_groups=mesh['batch'=2,'member'=16,'tensor'=4] {'tensor'}, use_global_device_ids=true, to_apply=%region_4.5 | all-reduce | flops 1024 | bytes 8192 | tf_op jit(solution)/shard_map/psum | solution.py:33
  360.7 0.6 dynamic_slice.3
  361.3 0.0 reduce-scatter.6.cloned.1.call-done
  361.3 3.5 copy.8
  364.8 0.0 reduce-scatter.8.cloned.1.call-done
  (1 shorter events, 0.0 us)
Async XLA Ops:
  7.2 81.5 %copy-start = (bf16[1,1024,1536]{2,1,0:T(8,128)(2,1)S(1)}, bf16[1,1024,1536]{2,1,0:T(8,128)(2,1)}, u32[]{:S(2)}) copy-start(bf16[1,1024,1536]{2,1,0:T(8,128)(2,1)} %param.7) | copy-start | bytes 9437188
  7.2 73.3 %all-gather.3.cloned.1.call-start = ((), (), s32[]{:S(2)}) async-start(), calls=%async_computation.3 | async-start | bytes 3194880 | tf_op jit(solution)/shard_map/all_gather | solution.py:14
  7.9 148.1 %reduce-scatter.4.cloned.1.call-start = ((), (), s32[]{:S(2)}) async-start(), calls=%async_computation.4 | async-start | bytes 7864320 | tf_op jit(solution)/shard_map/reduce_scatter | solution.py:24
  86.7 1.9 copy-start.2
  94.2 64.4 %copy-start.1 = (bf16[64,384]{1,0:T(8,128)(2,1)S(1)}, bf16[64,384]{1,0:T(8,128)(2,1)}, u32[]{:S(2)}) copy-start(bf16[64,384]{1,0:T(8,128)(2,1)} %param.5) | copy-start | bytes 147460
  94.2 152.1 %all-reduce.2.cloned.1.call-start = ((), (), s32[]{:S(2)}) async-start(), calls=%async_computation.5 | async-start | bytes 1572864 | tf_op jit(solution)/shard_map/psum | solution.py:30
  158.5 130.2 %all-gather.5.cloned.1.call-start = ((), (), s32[]{:S(2)}) async-start(), calls=%async_computation.6 | async-start | bytes 3932160 | tf_op jit(solution)/shard_map/all_gather | solution.py:28
  249.4 111.8 %reduce-scatter.6.cloned.1.call-start = ((), (), s32[]{:S(2)}) async-start(), calls=%async_computation.7 | async-start | bytes 9437184 | tf_op jit(solution)/shard_map/reduce_scatter | solution.py:43
  302.3 62.5 %reduce-scatter.8.cloned.1.call-start = ((), (), s32[]{:S(2)}) async-start(), calls=%async_computation.8 | async-start | bytes 9437184 | tf_op jit(solution)/shard_map/reduce_scatter | solution.py:44
Sparse Core Ops, SparseCore 0:
  10.9 69.5 all-gather.2
  94.3 61.7 reduce-scatter.3
  159.9 86.3 all-reduce.1
  249.5 39.0 all-gather.4
  302.4 17.1 reduce-scatter.5
  322.5 18.5 reduce-scatter.7
